TPU v7x, 256 devices: a whole 4x4x8 slice. The times are simulated.
256 devices in a mesh: outer: 16 (over z, x_hi), inner: 16 (over x_lo, y, core).
Axes of the slice: x: 4 (x_hi: 2, x_lo: 2; x = x_hi * 2 + x_lo), y: 4, z: 8, core: 2. Of those that a mesh axis runs over, the one named last changes fastest.
Arguments:
- user_factors: float32 [131072, 256], P(('outer', 'inner')), may hold values from -0.3 to 0.3
- item_factors: float32 [131072, 256], P(('outer', 'inner')), may hold values from -0.3 to 0.3
- ratings: bfloat16 [131072, 8, 512], P(('outer', 'inner')), may hold values from -6 to 6
- weights: bfloat16 [131072, 8, 512], P(('outer', 'inner')), may hold values from 0 to 2, as said below
- tile_list: int32 [256, 8, 4], P(('outer', 'inner')), may hold values from 0 to 3, as said below
- tile_count: int32 [256, 8], P(('outer', 'inner')), may hold values from 1 to 4, as said below
Outputs:
- users_out: float32 [131072, 256], P(('outer', 'inner'))
- items_out: float32 [131072, 256], P(('outer', 'inner'))
Inputs may be any that keep to these rules, and one draw needn't show every extreme that they name: Every row tile_list[d,k,:] names each of 0 to 3 once. `tile_count`: in every draw some device lists all 4 tiles in some stratum. `weights`: zero outside the listed tiles and at unobserved entries; elsewhere between 0.5 and 2.
All inputs are finite; a program needn't handle non-finite values.
Results may differ from a plain program's by a relative error of at most 0.003.
Values sent between devices are 32-bit elements; how exact they have to be, the bound alone decides.
A program may use at most 64 MiB of HBM per device.

v0:
```python
import jax
import jax.numpy as jnp
from jax import lax
from jax.sharding import PartitionSpec as P

S_OUT = 2
S_IN = 4


learn_rate = 0.015
ridge_weight = 0.05


def from_behind(value, axis, steps):
    count = lax.axis_size(axis)
    pairs = [(source, (source + steps) % count) for source in range(count)]
    return lax.ppermute(value, axis, pairs)


def listed_mask(order_row, count, tile_total, tile_width):
    slot_ids = jnp.arange(tile_total, dtype=jnp.int32)
    matched = (order_row[:, None] == slot_ids[None, :]) & (slot_ids[:, None] < count)
    return jnp.repeat(jnp.any(matched, axis=0).astype(jnp.float32), tile_width)


def move_items(item_rows, outer_step, inner_step):
    if inner_step < S_IN - 1:
        return from_behind(item_rows, "inner", 1)
    if outer_step < S_OUT - 1:
        return from_behind(item_rows, "outer", 1)
    return item_rows


def local(user_factors, item_factors, ratings, weights, tile_list, tile_count):
    tile_total = tile_list.shape[2]
    tile_width = item_factors.shape[0] // tile_total
    user_rows = user_factors
    item_rows = item_factors
    contract_rank = (((1,), (1,)), ((), ()))
    contract_users = (((0,), (0,)), ((), ()))
    for outer_step in range(S_OUT):
        for inner_step in range(S_IN):
            stratum = outer_step * S_IN + inner_step
            rating = ratings[:, stratum, :]
            weight = weights[:, stratum, :]
            order_row = tile_list[0, stratum]
            count = tile_count[0, stratum]
            user_half = user_rows.astype(jnp.bfloat16)
            item_half = item_rows.astype(jnp.bfloat16)
            tile_mask = listed_mask(order_row, count, tile_total, tile_width)
            predicted = lax.dot_general(
                user_half, item_half, contract_rank, preferred_element_type=jnp.float32
            )
            residual = (
                weight.astype(jnp.float32)
                * (predicted - rating.astype(jnp.float32))
                * tile_mask[None, :]
            ).astype(jnp.bfloat16)
            grad_items = lax.dot_general(
                residual, user_half, contract_users, preferred_element_type=jnp.float32
            )

            def users_grad(residual=residual, item_half=item_half):
                return jnp.dot(residual, item_half, preferred_element_type=jnp.float32)

            new_items = item_rows - learn_rate * (grad_items + ridge_weight * item_rows)
            user_rows = user_rows - learn_rate * (users_grad() + ridge_weight * user_rows)
            item_rows = move_items(new_items, outer_step, inner_step)
    return (user_rows, item_rows)


def solution(mesh):
    in_specs = (
        P(("outer", "inner"), None),
        P(("outer", "inner"), None),
        P(("outer", "inner"), None, None),
        P(("outer", "inner"), None, None),
        P(("outer", "inner"), None, None),
        P(("outer", "inner"), None),
    )
    out_specs = (P(("outer", "inner"), None), P(("outer", "inner"), None))
    return jax.shard_map(local, mesh=mesh, in_specs=in_specs, out_specs=out_specs, check_vma=False)
```

profile of v0, /device:TPU:2, one launch (start us, length us, event | category | flops | bytes accessed | tf_op | source)
XLA Modules:
  0.0 133.4 jit_solution(3913745748496496729)
XLA Ops:
  0.6 1.6 %fusion.113 = (s32[1,1]{1,0:T(1,128)}, s32[1,1]{1,0:T(1,128)}, s32[1,1]{1,0:T(1,128)}, s32[1,1]{1,0:T(1,128)}, s32[1,1]{1,0:T(1,128)}, /*index=5*/s32[1,1]{1,0:T(1,128)}, s32[1,1]{1,0:T(1,128)}, s32[1,1]{1,0:T(1,128)}) fusion(s32[1,8]{1,0:T(1,128)} %param.11), kind=kLoop, calls=%fused_computation.171 | loop fusion | bytes 64 | tf_op jit(solution)/shard_map/slice | solution.py:47
  2.3 0.7 iota_compare_fusion.14
  3.0 0.6 iota_compare_fusion.15
  3.5 1.3 slice_reduce_fusion
  5.0 39.2 %fusion.111 = (bf16[512,1,512]{2,1,0:T(2,128)(2,1)S(1)}, bf16[512,1,512]{2,1,0:T(2,128)(2,1)S(1)}, bf16[512,1,512]{2,1,0:T(2,128)(2,1)S(1)}, bf16[512,1,512]{2,1...) fusion(bf16[512,8,512]{2,1,0:T(8,128)(2,1)} %param.9, ...), kind=kLoop, calls=%fused_computation.169 | loop fusion | bytes 16777216 | tf_op jit(solution)/shard_map/slice | solution.py:45
  44.2 2.1 %fusion.23 = bf16[512,512]{1,0:T(8,128)(2,1)S(1)} fusion(bf16[512,1,512]{2,1,0:T(2,128)(2,1)} %get-tuple-element.42, bf16[512,1,512]{2,1,0:T(2,128)(2,1)} %get-tuple-element.17, f32[512]{0:T(512)S(1)} %broadcast_bitcast_fusion.7, f32[512,256]{1,0:T(8,128)S(1)} %copy-done.1, f32[512,256]{1,0:T(8,128)S(1)} %copy-done), kind=kOutput, calls=%fused_computation.31 | convolution fusion | flops 136052736 | bytes 2623488 | tf_op jit(solution)/shard_map/dot_general | solution.py:51
  46.7 0.7 iota_compare_fusion.12
  47.4 0.6 iota_compare_fusion.13
  48.1 0.6 iota_compare_fusion.10
  49.2 8.3 %collective-permute-done = f32[512,256]{1,0:T(8,128)S(1)} collective-permute-done((f32[512,256]{1,0:T(8,128)S(1)}, f32[512,256]{1,0:T(8,128)S(1)}, u32[]{:S(2)}, u32[]{:S(2)}) %collective-permute-start) | collective-permute-done | bytes 524320 | tf_op jit(solution)/shard_map/ppermute | solution.py:17
  57.4 0.4 fusion.22
  58.3 0.6 iota_compare_fusion.11
  59.3 9.7 %collective-permute-done.1 = f32[512,256]{1,0:T(8,128)S(1)} collective-permute-done((f32[512,256]{1,0:T(8,128)S(1)}, f32[512,256]{1,0:T(8,128)S(1)}, u32[]{:S(2)}, u32[]{:S(2)}) %collective-permute-start.1) | collective-permute-done | bytes 524320 | tf_op jit(solution)/shard_map/ppermute | solution.py:17
  70.3 10.2 %collective-permute-done.2 = f32[512,256]{1,0:T(8,128)S(1)} collective-permute-done((f32[512,256]{1,0:T(8,128)S(1)}, f32[512,256]{1,0:T(8,128)S(1)}, u32[]{:S(2)}, u32[]{:S(2)}) %collective-permute-start.2) | collective-permute-done | bytes 524320 | tf_op jit(solution)/shard_map/ppermute | solution.py:17
  81.3 2.4 %collective-permute-start.3 = (f32[512,256]{1,0:T(8,128)S(1)}, f32[512,256]{1,0:T(8,128)S(1)}, u32[]{:S(2)}, u32[]{:S(2)}) collective-permute-start(f32[512,256]{1,0:T(8,128)S(1)} %multiply_subtract_fusion.4), channel_id=1, source_target_pairs={{0,16},{16,32},{32,48},{48,64},{64,80},{80,96},{96,112},{112,128},... | collective-permute-start | bytes 1572872 | tf_op jit(solution)/shard_map/ppermute | solution.py:17
  83.7 0.6 iota_compare_fusion.8
  84.7 11.4 %collective-permute-done.3 = f32[512,256]{1,0:T(8,128)S(1)} collective-permute-done((f32[512,256]{1,0:T(8,128)S(1)}, f32[512,256]{1,0:T(8,128)S(1)}, u32[]{:S(2)}, u32[]{:S(2)}) %collective-permute-start.3) | collective-permute-done | bytes 524320 | tf_op jit(solution)/shard_map/ppermute | solution.py:17
  96.1 0.4 fusion.19
  97.0 0.6 iota_compare_fusion.9
  98.0 9.7 %collective-permute-done.4 = f32[512,256]{1,0:T(8,128)S(1)} collective-permute-done((f32[512,256]{1,0:T(8,128)S(1)}, f32[512,256]{1,0:T(8,128)S(1)}, u32[]{:S(2)}, u32[]{:S(2)}) %collective-permute-start.4) | collective-permute-done | bytes 524320 | tf_op jit(solution)/shard_map/ppermute | solution.py:17
  109.0 10.2 %collective-permute-done.5 = f32[512,256]{1,0:T(8,128)S(1)} collective-permute-done((f32[512,256]{1,0:T(8,128)S(1)}, f32[512,256]{1,0:T(8,128)S(1)}, u32[]{:S(2)}, u32[]{:S(2)}) %collective-permute-start.5) | collective-permute-done | bytes 524320 | tf_op jit(solution)/shard_map/ppermute | solution.py:17
  120.5 10.3 %collective-permute-done.6 = f32[512,256]{1,0:T(8,128)S(1)} collective-permute-done((f32[512,256]{1,0:T(8,128)S(1)}, f32[512,256]{1,0:T(8,128)S(1)}, u32[]{:S(2)}, u32[]{:S(2)}) %collective-permute-start.6) | collective-permute-done | bytes 524320 | tf_op jit(solution)/shard_map/ppermute | solution.py:17
  131.2 1.1 multiply_subtract_fusion
  132.3 1.1 fusion.25
  (55 shorter events, 8.0 us)
Async XLA Ops:
  5.0 39.2 %copy-start = (f32[512,256]{1,0:T(8,128)S(1)}, f32[512,256]{1,0:T(8,128)}, u32[]{:S(2)}) copy-start(f32[512,256]{1,0:T(8,128)} %param.6) | copy-start | bytes 1572868
  5.0 39.2 %copy-start.1 = (f32[512,256]{1,0:T(8,128)S(1)}, f32[512,256]{1,0:T(8,128)}, u32[]{:S(2)}) copy-start(f32[512,256]{1,0:T(8,128)} %param.7) | copy-start | bytes 1572868
  44.2 13.3 %copy-start.3 = (bf16[512,1,512]{2,1,0:T(2,128)(2,1)S(1)}, bf16[512,1,512]{2,1,0:T(2,128)(2,1)}, u32[]{:S(2)}) copy-start(bf16[512,1,512]{2,1,0:T(2,128)(2,1)} %get-tuple-element.16) | copy-start | bytes 1572868
  44.2 13.3 %copy-start.4 = (bf16[512,1,512]{2,1,0:T(2,128)(2,1)S(1)}, bf16[512,1,512]{2,1,0:T(2,128)(2,1)}, u32[]{:S(2)}) copy-start(bf16[512,1,512]{2,1,0:T(2,128)(2,1)} %get-tuple-element.43) | copy-start | bytes 1572868
  46.6 10.8 %collective-permute-start = (f32[512,256]{1,0:T(8,128)S(1)}, f32[512,256]{1,0:T(8,128)S(1)}, u32[]{:S(2)}, u32[]{:S(2)}) collective-permute-start(f32[512,256]{1,0:T(8,128)S(1)} %fusion.39), channel_id=1, source_target_pairs={{0,1},{1,2},{2,3},{3,4},{4,5},{5,6},{6,7},{7,8},{8,9},{9,10},{10,1... | collective-permute-start | bytes 1572872 | tf_op jit(solution)/shard_map/ppermute | solution.py:17
  48.9 20.1 %copy-start.2 = (bf16[512,1,512]{2,1,0:T(2,128)(2,1)S(1)}, bf16[512,1,512]{2,1,0:T(2,128)(2,1)}, u32[]{:S(2)}) copy-start(bf16[512,1,512]{2,1,0:T(2,128)(2,1)} %get-tuple-element.44) | copy-start | bytes 1572868
  58.2 10.8 %collective-permute-start.1 = (f32[512,256]{1,0:T(8,128)S(1)}, f32[512,256]{1,0:T(8,128)S(1)}, u32[]{:S(2)}, u32[]{:S(2)}) collective-permute-start(f32[512,256]{1,0:T(8,128)S(1)} %multiply_subtract_fusion.6), channel_id=1, source_target_pairs={{0,1},{1,2},{2,3},{3,4},{4,5},{5,6},{6,7},{7,8},{8,9},{9,10},{10,1... | collective-permute-start | bytes 1572872 | tf_op jit(solution)/shard_map/ppermute | solution.py:17
  69.8 10.8 %collective-permute-start.2 = (f32[512,256]{1,0:T(8,128)S(1)}, f32[512,256]{1,0:T(8,128)S(1)}, u32[]{:S(2)}, u32[]{:S(2)}) collective-permute-start(f32[512,256]{1,0:T(8,128)S(1)} %multiply_subtract_fusion.5), channel_id=1, source_target_pairs={{0,1},{1,2},{2,3},{3,4},{4,5},{5,6},{6,7},{7,8},{8,9},{9,10},{10,1... | collective-permute-start | bytes 1572872 | tf_op jit(solution)/shard_map/ppermute | solution.py:17
  81.3 14.8 %collective-permute-start.3 = (f32[512,256]{1,0:T(8,128)S(1)}, f32[512,256]{1,0:T(8,128)S(1)}, u32[]{:S(2)}, u32[]{:S(2)}) collective-permute-start(f32[512,256]{1,0:T(8,128)S(1)} %multiply_subtract_fusion.4), channel_id=1, source_target_pairs={{0,16},{16,32},{32,48},{48,64},{64,80},{80,96},{96,112},{112,128},... | collective-permute-start | bytes 1572872 | tf_op jit(solution)/shard_map/ppermute | solution.py:17
  96.9 10.8 %collective-permute-start.4 = (f32[512,256]{1,0:T(8,128)S(1)}, f32[512,256]{1,0:T(8,128)S(1)}, u32[]{:S(2)}, u32[]{:S(2)}) collective-permute-start(f32[512,256]{1,0:T(8,128)S(1)} %multiply_subtract_fusion.3), channel_id=1, source_target_pairs={{0,1},{1,2},{2,3},{3,4},{4,5},{5,6},{6,7},{7,8},{8,9},{9,10},{10,1... | collective-permute-start | bytes 1572872 | tf_op jit(solution)/shard_map/ppermute | solution.py:17
  108.4 10.8 %collective-permute-start.5 = (f32[512,256]{1,0:T(8,128)S(1)}, f32[512,256]{1,0:T(8,128)S(1)}, u32[]{:S(2)}, u32[]{:S(2)}) collective-permute-start(f32[512,256]{1,0:T(8,128)S(1)} %multiply_subtract_fusion.2), channel_id=1, source_target_pairs={{0,1},{1,2},{2,3},{3,4},{4,5},{5,6},{6,7},{7,8},{8,9},{9,10},{10,1... | collective-permute-start | bytes 1572872 | tf_op jit(solution)/shard_map/ppermute | solution.py:17
  120.0 10.8 %collective-permute-start.6 = (f32[512,256]{1,0:T(8,128)S(1)}, f32[512,256]{1,0:T(8,128)S(1)}, u32[]{:S(2)}, u32[]{:S(2)}) collective-permute-start(f32[512,256]{1,0:T(8,128)S(1)} %multiply_subtract_fusion.1), channel_id=1, source_target_pairs={{0,1},{1,2},{2,3},{3,4},{4,5},{5,6},{6,7},{7,8},{8,9},{9,10},{10,1... | collective-permute-start | bytes 1572872 | tf_op jit(solution)/shard_map/ppermute | solution.py:17
where the time goes:
time: 134 us; the launch traced here: 133 us
  waiting for transfers between devices  69.8 us (52%)
  local copies, waits for them, and re-layouts  42.7 us (32%)
  matrix products  11.6 us (9%)
  other arithmetic  5.51 us (4%)
  starting transfers between devices  2.88 us (2%)
    ppermute x7, waiting for transfers between devices, from_behind(): return lax.ppermute(value, axis, pairs)  69.8 us
    slice x1, local copies, waits for them, and re-layouts, local(): weight = weights[:, stratum, :]  39.2 us
    lt x8, other arithmetic, listed_mask(): slot_ids[:, None] < count  5.1 us
    dot_general x8, matrix products, local(): lax.dot_general(user_half, item_half, contract_rank, preferred_element_ty...  4.87 us
    dot_general x8, matrix products, local(): lax.dot_general(residual, user_half, contract_users, preferred_element_ty...  3.52 us
    dot_general x8, matrix products, users_grad(): return jnp.dot(residual, item_half, preferred_element_type=jnp.float32)  3.2 us
    ppermute x7, starting transfers between devices, from_behind(): return lax.ppermute(value, axis, pairs)  2.88 us
  transfers between devices with their start and end apart: 7, of which 7 were waited for; matrix products, arithmetic and copies ran while one was open for 5% of the time, Pallas kernels for 0%

commit v1 on v0

v1 whole, which is shorter than its diff:
```python
import functools

import jax
import jax.numpy as jnp
from jax import lax
from jax.experimental import pallas as pl
from jax.experimental.pallas import tpu as pltpu
from jax.sharding import PartitionSpec as P

S_OUT = 2
S_IN = 4
STRATA = S_OUT * S_IN
GROUP = 32
PIECES = 2

learn_rate = 0.015
ridge_weight = 0.05

MESH = pl.DeviceIdType.MESH


def listed_scales(list_ref, count_ref, stratum, tile_total):
    count = count_ref[0, stratum]
    scales = []
    for tile in range(tile_total):
        hits = [
            jnp.where(
                (list_ref[0, stratum, slot] == tile) & (slot < count), 1.0, 0.0
            ).astype(jnp.float32)
            for slot in range(tile_total)
        ]
        scales.append(functools.reduce(jnp.maximum, hits))
    return scales


def kernel(
    outer_size,
    inner_size,
    list_ref,
    count_ref,
    user_hbm,
    item_hbm,
    rating_hbm,
    weight_hbm,
    user_out,
    item_out,
    raw,
    sorted_rows,
    user,
    user_half,
    grad_user,
    held,
    fresh,
    load_sem,
    factor_sem,
    send_sem,
    recv_sem,
):
    users, rank = user.shape
    items = held.shape[1]
    width = items // PIECES
    tile_total = list_ref.shape[2]
    tile_width = items // tile_total
    groups = users // GROUP
    group_rows = GROUP * STRATA

    g = lax.axis_index("outer")
    i = lax.axis_index("inner")

    def along(steps_outer, steps_inner):
        return (
            lax.rem(g + steps_outer + outer_size, outer_size),
            lax.rem(i + steps_inner + inner_size, inner_size),
        )

    def load(group, which):
        rows = pl.ds(pl.multiple_of(group * group_rows, group_rows), group_rows)
        source = (rating_hbm, weight_hbm)[which]
        return pltpu.make_async_copy(
            source.at[rows], raw.at[which, rows], load_sem.at[which, group]
        )

    def load_all(group, carry):
        load(group, 0).start()
        load(group, 1).start()
        return carry

    user_load = pltpu.make_async_copy(user_hbm, user, factor_sem.at[0])
    item_load = pltpu.make_async_copy(item_hbm, held.at[0], factor_sem.at[1])
    user_load.start()
    item_load.start()
    lax.fori_loop(0, groups, load_all, 0)

    barrier = pltpu.get_barrier_semaphore()
    for partner in (along(0, 1), along(0, -1), along(1, 0), along(-1, 0)):
        pl.semaphore_signal(barrier, inc=1, device_id=partner, device_id_type=MESH)

    row_id = lax.broadcasted_iota(jnp.int32, (group_rows, group_rows), 0)
    col_id = lax.broadcasted_iota(jnp.int32, (group_rows, group_rows), 1)
    wanted = (row_id % GROUP) * STRATA + row_id // GROUP
    picks = jnp.where(col_id == wanted, 1.0, 0.0).astype(jnp.bfloat16)

    def sort_group(group, carry):
        rows = pl.ds(pl.multiple_of(group * group_rows, group_rows), group_rows)
        there = pl.ds(pl.multiple_of(group * GROUP, GROUP), GROUP)
        for which in range(2):
            load(group, which).wait()
            by_stratum = jnp.dot(
                picks, raw[which, rows, :], preferred_element_type=jnp.float32
            ).astype(jnp.bfloat16)
            for stratum in range(STRATA):
                sorted_rows[which, stratum, there, :] = by_stratum[
                    stratum * GROUP : (stratum + 1) * GROUP
                ]
        return carry

    lax.fori_loop(0, groups, sort_group, 0)
    user_load.wait()
    item_load.wait()
    user_half[...] = user[...].astype(jnp.bfloat16)
    pl.semaphore_wait(barrier, 4)

    def move(stratum, piece):
        is_outer = (stratum == S_IN - 1).astype(jnp.int32)
        rows = pl.ds(piece * width, width)
        return pltpu.make_async_remote_copy(
            src_ref=fresh.at[stratum, rows],
            dst_ref=held.at[stratum + 1, rows],
            send_sem=send_sem.at[stratum, piece],
            recv_sem=recv_sem.at[stratum, piece],
            device_id=along(is_outer, 1 - is_outer),
            device_id_type=MESH,
        )

    def work(stratum, first, last):
        scales = listed_scales(list_ref, count_ref, stratum, tile_total)
        column = lax.broadcasted_iota(jnp.int32, (1, width), 1)
        for piece in range(PIECES):
            rows = slice(piece * width, (piece + 1) * width)
            if not first:
                move(stratum - 1, piece).wait_recv()
            item = held[stratum, rows, :]
            item_half = item.astype(jnp.bfloat16)
            listed = jnp.zeros((1, width), jnp.float32)
            for tile in range(width // tile_width):
                listed = jnp.where(
                    column >= tile * tile_width,
                    scales[piece * width // tile_width + tile],
                    listed,
                )
            predicted = lax.dot_general(
                user_half[...],
                item_half,
                (((1,), (1,)), ((), ())),
                preferred_element_type=jnp.float32,
            )
            rating = sorted_rows[0, stratum, :, rows].astype(jnp.float32)
            weight = sorted_rows[1, stratum, :, rows].astype(jnp.float32)
            residual = (weight * (predicted - rating) * listed).astype(jnp.bfloat16)
            grad_item = lax.dot_general(
                residual,
                user_half[...],
                (((0,), (0,)), ((), ())),
                preferred_element_type=jnp.float32,
            )
            fresh[stratum, rows, :] = item - learn_rate * (grad_item + ridge_weight * item)
            if last:
                pltpu.make_async_copy(
                    fresh.at[stratum, rows], item_out.at[rows], send_sem.at[stratum, piece]
                ).start()
            else:
                move(stratum, piece).start()
            part = jnp.dot(residual, item_half, preferred_element_type=jnp.float32)
            if piece == 0:
                grad_user[...] = part
            else:
                part = grad_user[...] + part
                if piece < PIECES - 1:
                    grad_user[...] = part
                else:
                    old = user[...]
                    new = old - learn_rate * (part + ridge_weight * old)
                    user[...] = new
                    if not last:
                        user_half[...] = new.astype(jnp.bfloat16)

    work(jnp.int32(0), True, False)

    def middle(stratum, carry):
        work(stratum, False, False)
        return carry

    lax.fori_loop(1, STRATA - 1, middle, 0)
    work(jnp.int32(STRATA - 1), False, True)

    user_store = pltpu.make_async_copy(user, user_out, factor_sem.at[0])
    user_store.start()
    for piece in range(PIECES):
        rows = slice(piece * width, (piece + 1) * width)
        pltpu.make_async_copy(
            fresh.at[STRATA - 1, rows], item_out.at[rows], send_sem.at[STRATA - 1, piece]
        ).wait()

    def sent(stratum, carry):
        for piece in range(PIECES):
            move(stratum, piece).wait_send()
        return carry

    lax.fori_loop(0, STRATA - 1, sent, 0)
    user_store.wait()


def local(outer_size, inner_size, user_factors, item_factors, ratings, weights, tile_list, tile_count):
    users, strata, items = ratings.shape
    rank = user_factors.shape[1]
    smem = pl.BlockSpec(memory_space=pltpu.SMEM)
    anywhere = pl.BlockSpec(memory_space=pl.ANY)
    block = jax.ShapeDtypeStruct((users, rank), jnp.float32)
    return pl.pallas_call(
        functools.partial(kernel, outer_size, inner_size),
        out_shape=(block, jax.ShapeDtypeStruct((items, rank), jnp.float32)),
        in_specs=[smem, smem, anywhere, anywhere, anywhere, anywhere],
        out_specs=(anywhere, anywhere),
        scratch_shapes=[
            pltpu.VMEM((2, users * strata, items), jnp.bfloat16),
            pltpu.VMEM((2, strata, users, items), jnp.bfloat16),
            pltpu.VMEM((users, rank), jnp.float32),
            pltpu.VMEM((users, rank), jnp.bfloat16),
            pltpu.VMEM((users, rank), jnp.float32),
            pltpu.VMEM((strata, items, rank), jnp.float32),
            pltpu.VMEM((strata, items, rank), jnp.float32),
            pltpu.SemaphoreType.DMA((2, users // GROUP)),
            pltpu.SemaphoreType.DMA((2,)),
            pltpu.SemaphoreType.DMA((strata, PIECES)),
            pltpu.SemaphoreType.DMA((strata, PIECES)),
        ],
        compiler_params=pltpu.CompilerParams(
            collective_id=0,
            has_side_effects=True,
            vmem_limit_bytes=48 * 1024 * 1024,
        ),
        cost_estimate=pl.CostEstimate(
            flops=3 * 2 * strata * users * items * rank,
            bytes_accessed=4 * users * strata * items + 16 * users * rank,
            transcendentals=0,
        ),
    )(
        tile_list,
        tile_count,
        user_factors,
        item_factors,
        ratings.reshape(users * strata, items),
        weights.reshape(users * strata, items),
    )


def solution(mesh):
    in_specs = (
        P(("outer", "inner"), None),
        P(("outer", "inner"), None),
        P(("outer", "inner"), None, None),
        P(("outer", "inner"), None, None),
        P(("outer", "inner"), None, None),
        P(("outer", "inner"), None),
    )
    out_specs = (P(("outer", "inner"), None), P(("outer", "inner"), None))
    return jax.shard_map(
        functools.partial(local, mesh.shape["outer"], mesh.shape["inner"]),
        mesh=mesh,
        in_specs=in_specs,
        out_specs=out_specs,
        check_vma=False,
    )
```

time: 134 us -> 75 us (0.56)
  the two profiles are of different devices: /device:TPU:2 before, /device:TPU:8 now
where the time goes in v1:
time: 75 us; the launch traced here: 74.8 us
  Pallas kernels  69.1 us (92%)
  local copies, waits for them, and re-layouts  5.08 us (7%)
    pallas_call x1, Pallas kernels, local(): pl.pallas_call(functools.partial(kernel, outer_size, inner_size), out_sha...  69.1 us
    unnamed x9, local copies, waits for them, and re-layouts  5.08 us

profile of v1, /device:TPU:8, one launch (start us, length us, event | category | flops | bytes accessed | tf_op | source)
XLA Modules:
  0.0 74.8 jit_solution(3191990197400714440)
XLA Ops:
  0.6 0.8 %copy.8.list_ref = s32[1,8,4]{2,1,0:T(8,128)S(1)} copy(s32[1,8,4]{1,2,0:T(4,128)} %param.10) | data formatting | bytes 256 | tf_op args[4]
  1.4 0.0 copy-start
  1.4 1.0 %copy-done = f32[512,256]{1,0:T(8,128)S(1)} copy-done((f32[512,256]{1,0:T(8,128)S(1)}, f32[512,256]{1,0:T(8,128)}, u32[]{:S(2)}) %copy-start) | copy-done | bytes 524312
  2.4 0.0 copy-start.1
  2.4 1.0 %copy-done.1 = f32[512,256]{1,0:T(8,128)S(1)} copy-done((f32[512,256]{1,0:T(8,128)S(1)}, f32[512,256]{1,0:T(8,128)}, u32[]{:S(2)}) %copy-start.1) | copy-done | bytes 524312
  3.5 0.0 copy-start.2
  3.5 0.7 copy-done.2
  4.1 69.1 %shard_map.77 = (f32[512,256]{1,0:T(8,128)S(1)}, f32[512,256]{1,0:T(8,128)S(1)}) custom-call(s32[1,8,4]{2,1,0:T(8,128)S(1)} %copy.8.list_ref, s32[1,8]{1,0:T(1,128)S(1)} %copy-done.2, f32[512,256]{1,0:T(8,128)S(1)} %copy-done, f32[512,256]{1,0:T(8,128)S(1)} %copy-done.1, bf16[4096,512]{1,0:T(8,128)(2,1)} %bitcast.2, bf16[4096,512]{1,0:T(8,128)(2,1)} %bitcast.3), custom_call_target="tpu_custom_call" | custom-call | flops 3221225472 | bytes 10485760 | tf_op jit(solution)/shard_map/pallas_call | solution.py:219
  73.2 0.8 %copy.11 = f32[512,256]{1,0:T(8,128)} copy(f32[512,256]{1,0:T(8,128)S(1)} %get-tuple-element.4) | data formatting | bytes 1048576
  74.0 0.8 %copy.12 = f32[512,256]{1,0:T(8,128)} copy(f32[512,256]{1,0:T(8,128)S(1)} %get-tuple-element.5) | data formatting | bytes 1048576
Async XLA Ops:
  1.4 1.0 %copy-start = (f32[512,256]{1,0:T(8,128)S(1)}, f32[512,256]{1,0:T(8,128)}, u32[]{:S(2)}) copy-start(f32[512,256]{1,0:T(8,128)} %user_hbm.1) | copy-start | bytes 1572868
  2.4 1.0 %copy-start.1 = (f32[512,256]{1,0:T(8,128)S(1)}, f32[512,256]{1,0:T(8,128)}, u32[]{:S(2)}) copy-start(f32[512,256]{1,0:T(8,128)} %item_hbm.1) | copy-start | bytes 1572868
  3.5 0.7 copy-start.2

commit v2 on v1

v2 whole, which is shorter than its diff:
```python
import functools

import jax
import jax.numpy as jnp
from jax import lax
from jax.experimental import pallas as pl
from jax.experimental.pallas import tpu as pltpu
from jax.sharding import PartitionSpec as P

S_OUT = 2
S_IN = 4
STRATA = S_OUT * S_IN
GROUP = 32
CHIPS = 4
CORES = 2
PIECES = 2
PARTS = 4

learn_rate = 0.015
ridge_weight = 0.05

MESH = pl.DeviceIdType.MESH


def listed_scales(list_ref, count_ref, stratum, tile_total):
    count = count_ref[0, stratum]
    scales = []
    for tile in range(tile_total):
        hits = [
            jnp.where(
                (list_ref[0, slot, stratum] == tile) & (slot < count), 1.0, 0.0
            ).astype(jnp.float32)
            for slot in range(tile_total)
        ]
        scales.append(functools.reduce(jnp.maximum, hits))
    return scales


def kernel(
    outer_size,
    inner_size,
    list_hbm,
    count_hbm,
    user_hbm,
    item_hbm,
    rating_hbm,
    weight_hbm,
    user_out,
    item_out,
    list_ref,
    count_ref,
    raw,
    ordered,
    picks,
    user,
    user_half,
    grad_user,
    held,
    fresh,
    passing,
    load_sem,
    factor_sem,
    send_sem,
    recv_sem,
    pass_sem,
):
    users, rank = user.shape
    items = held.shape[1]
    width = items // PIECES
    tile_total = list_ref.shape[1]
    tile_width = items // tile_total
    groups = users // GROUP
    group_rows = GROUP * STRATA
    part_users = users // PARTS
    part_rows = part_users * STRATA

    g = lax.axis_index("outer")
    i = lax.axis_index("inner")

    run = CHIPS * CORES
    place = lax.rem(i, run)
    corner, stop = place == run - 1, place == run - 1 - CORES

    def along(steps_outer, steps_inner):
        return (
            lax.rem(g + steps_outer + outer_size, outer_size),
            lax.rem(i + steps_inner + inner_size, inner_size),
        )

    def load(which, piece, part):
        rows = pl.ds(part * part_rows, part_rows)
        cols = pl.ds(piece * width, width)
        source = (rating_hbm, weight_hbm)[which]
        return pltpu.make_async_copy(
            source.at[rows, cols], raw.at[which, rows, cols], load_sem.at[which, piece, part]
        )

    factor_loads = [
        pltpu.make_async_copy(list_hbm, list_ref, factor_sem.at[2]),
        pltpu.make_async_copy(count_hbm, count_ref, factor_sem.at[3]),
        pltpu.make_async_copy(user_hbm, user, factor_sem.at[0]),
        pltpu.make_async_copy(item_hbm, held.at[0], factor_sem.at[1]),
    ]
    for copy in factor_loads:
        copy.start()
    for piece in range(PIECES):
        for part in range(PARTS):
            load(0, piece, part).start()
            load(1, piece, part).start()

    barrier = pltpu.get_barrier_semaphore()
    for partner in (along(0, 1), along(0, -1), along(1, 0), along(-1, 0)):
        pl.semaphore_signal(barrier, inc=1, device_id=partner, device_id_type=MESH)

    @pl.when(corner)
    def greet_stop():
        pl.semaphore_signal(
            barrier, inc=1, device_id=along(-1, -CORES), device_id_type=MESH
        )

    @pl.when(stop)
    def greet_corner():
        pl.semaphore_signal(
            barrier, inc=1, device_id=along(0, CORES), device_id_type=MESH
        )

    def meet_all():
        @pl.when(corner | stop)
        def meet_five():
            pl.semaphore_wait(barrier, 5)

        @pl.when(jnp.logical_not(corner | stop))
        def meet_four():
            pl.semaphore_wait(barrier, 4)

    row_id = lax.broadcasted_iota(jnp.int32, (GROUP, group_rows), 0)
    col_id = lax.broadcasted_iota(jnp.int32, (GROUP, group_rows), 1)
    for stratum in range(STRATA):
        picks[stratum] = jnp.where(
            col_id == row_id * STRATA + stratum, 1.0, 0.0
        ).astype(jnp.bfloat16)

    def sort_part(stratum, part, cols):
        pick = picks[stratum]
        for group in range(groups // PARTS):
            base = part * part_rows + group * group_rows
            rows = pl.ds(pl.multiple_of(base, group_rows), group_rows)
            base = part * part_users + group * GROUP
            there = pl.ds(pl.multiple_of(base, GROUP), GROUP)
            for which in range(2):
                ordered[which, there, cols] = jnp.dot(
                    pick, raw[which, rows, cols], preferred_element_type=jnp.float32
                )

    def sort_all(stratum):
        def body(part, carry):
            sort_part(stratum, part, slice(None))
            return carry

        lax.fori_loop(0, PARTS, body, 0)

    def move(stratum, piece):
        is_outer = (stratum == S_IN - 1).astype(jnp.int32)
        rows = pl.ds(piece * width, width)
        return pltpu.make_async_remote_copy(
            src_ref=fresh.at[stratum, rows],
            dst_ref=held.at[stratum + 1, rows],
            send_sem=send_sem.at[stratum, piece],
            recv_sem=recv_sem.at[stratum, piece],
            device_id=along(is_outer, 1 - is_outer),
            device_id_type=MESH,
        )

    first_rows = pl.ds(0, width)
    turn = S_IN - 1

    def to_stop():
        return pltpu.make_async_remote_copy(
            src_ref=fresh.at[turn, first_rows],
            dst_ref=passing,
            send_sem=send_sem.at[turn, 0],
            recv_sem=pass_sem.at[0],
            device_id=along(0, -CORES),
            device_id_type=MESH,
        )

    def from_stop():
        return pltpu.make_async_remote_copy(
            src_ref=passing,
            dst_ref=held.at[turn + 1, first_rows],
            send_sem=pass_sem.at[1],
            recv_sem=recv_sem.at[turn, 0],
            device_id=along(1, CORES),
            device_id_type=MESH,
        )

    def send(stratum, piece):
        if piece == 0:
            around = corner & (stratum == turn)

            @pl.when(around)
            def send_around():
                to_stop().start()

            @pl.when(jnp.logical_not(around))
            def send_straight():
                move(stratum, piece).start()
        else:
            @pl.when((stratum == turn) & (place == run - 1))
            def yield_link():
                for earlier in range(PIECES):
                    move(stratum - 1, earlier).wait_send()

            move(stratum, piece).start()

    def work(stratum, first, last):
        scales = []
        if not first:
            scales.extend(listed_scales(list_ref, count_ref, stratum, tile_total))
        column = lax.broadcasted_iota(jnp.int32, (1, width), 1)
        for piece in range(PIECES):
            rows = slice(piece * width, (piece + 1) * width)
            if first:
                for part in range(PARTS):
                    load(0, piece, part).wait()
                    load(1, piece, part).wait()
                    sort_part(stratum, part, rows)
                if piece == 0:
                    for copy in factor_loads:
                        copy.wait()
                    user_half[...] = user[...].astype(jnp.bfloat16)
                    scales.extend(listed_scales(list_ref, count_ref, stratum, tile_total))
            else:
                move(stratum - 1, piece).wait_recv()
            item = held[stratum, rows, :]
            item_half = item.astype(jnp.bfloat16)
            listed = jnp.zeros((1, width), jnp.float32)
            for tile in range(width // tile_width):
                listed = jnp.where(
                    column >= tile * tile_width,
                    scales[piece * width // tile_width + tile],
                    listed,
                )
            predicted = lax.dot_general(
                user_half[...],
                item_half,
                (((1,), (1,)), ((), ())),
                preferred_element_type=jnp.float32,
            )
            rating = ordered[0, :, rows]
            weight = ordered[1, :, rows]
            residual = (weight * (predicted - rating) * listed).astype(jnp.bfloat16)
            grad_item = lax.dot_general(
                residual,
                user_half[...],
                (((0,), (0,)), ((), ())),
                preferred_element_type=jnp.float32,
            )
            fresh[stratum, rows, :] = item - learn_rate * (grad_item + ridge_weight * item)
            if last:
                pltpu.make_async_copy(
                    fresh.at[stratum, rows], item_out.at[rows], send_sem.at[stratum, piece]
                ).start()
            else:
                if first and piece == 0:
                    meet_all()
                send(stratum, piece)
            part = jnp.dot(residual, item_half, preferred_element_type=jnp.float32)
            if piece == 0:
                grad_user[...] = part
            else:
                part = grad_user[...] + part
                if piece < PIECES - 1:
                    grad_user[...] = part
                else:
                    old = user[...]
                    new = old - learn_rate * (part + ridge_weight * old)
                    user[...] = new
                    if not last:
                        user_half[...] = new.astype(jnp.bfloat16)
                        sort_all(stratum + 1)
                        if not first:

                            @pl.when(stop & (stratum == turn))
                            def pass_on():
                                to_stop().wait_recv()
                                from_stop().start()

    work(jnp.int32(0), True, False)

    def middle(stratum, carry):
        work(stratum, False, False)
        return carry

    lax.fori_loop(1, STRATA - 1, middle, 0)
    work(jnp.int32(STRATA - 1), False, True)

    user_store = pltpu.make_async_copy(user, user_out, factor_sem.at[0])
    user_store.start()
    for piece in range(PIECES):
        rows = slice(piece * width, (piece + 1) * width)
        pltpu.make_async_copy(
            fresh.at[STRATA - 1, rows], item_out.at[rows], send_sem.at[STRATA - 1, piece]
        ).wait()

    def sent(stratum, carry):
        @pl.when(jnp.logical_not((stratum == turn - 1) & (place == run - 1)))
        def settle():
            for piece in range(PIECES):
                move(stratum, piece).wait_send()

        return carry

    lax.fori_loop(0, STRATA - 1, sent, 0)

    @pl.when(stop)
    def settle_passed():
        from_stop().wait_send()

    user_store.wait()


def local(outer_size, inner_size, user_factors, item_factors, ratings, weights, tile_list, tile_count):
    users, strata, items = ratings.shape
    rank = user_factors.shape[1]
    anywhere = pl.BlockSpec(memory_space=pl.ANY)
    block = jax.ShapeDtypeStruct((users, rank), jnp.float32)
    return pl.pallas_call(
        functools.partial(kernel, outer_size, inner_size),
        out_shape=(block, jax.ShapeDtypeStruct((items, rank), jnp.float32)),
        in_specs=[anywhere] * 6,
        out_specs=(anywhere, anywhere),
        scratch_shapes=[
            pltpu.SMEM((1, tile_list.shape[2], strata), jnp.int32),
            pltpu.SMEM((1, strata), jnp.int32),
            pltpu.VMEM((2, users * strata, items), jnp.bfloat16),
            pltpu.VMEM((2, users, items), jnp.float32),
            pltpu.VMEM((strata, GROUP, GROUP * strata), jnp.bfloat16),
            pltpu.VMEM((users, rank), jnp.float32),
            pltpu.VMEM((users, rank), jnp.bfloat16),
            pltpu.VMEM((users, rank), jnp.float32),
            pltpu.VMEM((strata, items, rank), jnp.float32),
            pltpu.VMEM((strata, items, rank), jnp.float32),
            pltpu.VMEM((items // PIECES, rank), jnp.float32),
            pltpu.SemaphoreType.DMA((2, PIECES, PARTS)),
            pltpu.SemaphoreType.DMA((4,)),
            pltpu.SemaphoreType.DMA((strata, PIECES)),
            pltpu.SemaphoreType.DMA((strata, PIECES)),
            pltpu.SemaphoreType.DMA((2,)),
        ],
        compiler_params=pltpu.CompilerParams(
            collective_id=0,
            has_side_effects=True,
            vmem_limit_bytes=60 * 1024 * 1024,
        ),
        cost_estimate=pl.CostEstimate(
            flops=3 * 2 * strata * users * items * rank,
            bytes_accessed=4 * users * strata * items + 16 * users * rank,
            transcendentals=0,
        ),
    )(
        jnp.swapaxes(tile_list, 1, 2),
        tile_count,
        user_factors,
        item_factors,
        ratings.reshape(users * strata, items),
        weights.reshape(users * strata, items),
    )


def solution(mesh):
    in_specs = (
        P(("outer", "inner"), None),
        P(("outer", "inner"), None),
        P(("outer", "inner"), None, None),
        P(("outer", "inner"), None, None),
        P(("outer", "inner"), None, None),
        P(("outer", "inner"), None),
    )
    out_specs = (P(("outer", "inner"), None), P(("outer", "inner"), None))
    return jax.shard_map(
        functools.partial(local, mesh.shape["outer"], mesh.shape["inner"]),
        mesh=mesh,
        in_specs=in_specs,
        out_specs=out_specs,
        check_vma=False,
    )
```

time: 75 us -> 66 us (0.88)
  the two profiles are of different devices: /device:TPU:8 before, /device:TPU:2 now
where the time goes in v2:
time: 66 us; the launch traced here: 65.9 us
  Pallas kernels  61.5 us (93%)
  local copies, waits for them, and re-layouts  3.74 us (6%)
    pallas_call x1, Pallas kernels, local(): pl.pallas_call(functools.partial(kernel, outer_size, inner_size), out_sha...  61.5 us
    unnamed x2, local copies, waits for them, and re-layouts  3.74 us

profile of v2, /device:TPU:2, one launch (start us, length us, event | category | flops | bytes accessed | tf_op | source)
XLA Modules:
  0.0 65.9 jit_solution(14075874187398607057)
XLA Ops:
  0.6 61.5 %shard_map.77 = (f32[512,256]{1,0:T(8,128)}, f32[512,256]{1,0:T(8,128)}) custom-call(s32[1,4,8]{2,1,0:T(4,128)} %bitcast.5, s32[1,8]{1,0:T(1,128)} %count_hbm.1, f32[512,256]{1,0:T(8,128)} %user_hbm.1, f32[512,256]{1,0:T(8,128)} %item_hbm.1, bf16[4096,512]{1,0:T(8,128)(2,1)} %bitcast.3, bf16[4096,512]{1,0:T(8,128)(2,1)} %bitcast.4), custom_call_target="tpu_custom_call" | custom-call | flops 3221225472 | bytes 10485760 | tf_op jit(solution)/shard_map/pallas_call | solution.py:328
  62.1 1.9 %copy.10 = f32[512,256]{1,0:T(8,128)} copy(f32[512,256]{1,0:T(8,128)} %get-tuple-element.4) | data formatting | bytes 1048576
  64.0 1.9 %copy.11 = f32[512,256]{1,0:T(8,128)} copy(f32[512,256]{1,0:T(8,128)} %get-tuple-element.5) | data formatting | bytes 1048576

commit v3 on v2

--- a/solution.py
+++ b/solution.py
@@ -63,6 +63,7 @@
     send_sem,
     recv_sem,
     pass_sem,
+    go_sem,
 ):
     users, rank = user.shape
     items = held.shape[1]
@@ -194,8 +195,16 @@
             device_id_type=MESH,
         )
 
+    def clear():
+        pl.semaphore_signal(go_sem, inc=1, device_id=along(0, -1), device_id_type=MESH)
+
     def send(stratum, piece):
         if piece == 0:
+
+            @pl.when((stratum == turn) & ((place == run - 2) | (place == run - 4)))
+            def hold():
+                pl.semaphore_wait(go_sem, 1)
+
             around = corner & (stratum == turn)
 
             @pl.when(around)
@@ -256,12 +265,11 @@
                 (((0,), (0,)), ((), ())),
                 preferred_element_type=jnp.float32,
             )
-            fresh[stratum, rows, :] = item - learn_rate * (grad_item + ridge_weight * item)
+            renewed = item - learn_rate * (grad_item + ridge_weight * item)
             if last:
-                pltpu.make_async_copy(
-                    fresh.at[stratum, rows], item_out.at[rows], send_sem.at[stratum, piece]
-                ).start()
+                item_out[rows, :] = renewed
             else:
+                fresh[stratum, rows, :] = renewed
                 if first and piece == 0:
                     meet_all()
                 send(stratum, piece)
@@ -275,16 +283,25 @@
                 else:
                     old = user[...]
                     new = old - learn_rate * (part + ridge_weight * old)
-                    user[...] = new
-                    if not last:
+                    if last:
+                        user_out[...] = new
+                    else:
+                        user[...] = new
                         user_half[...] = new.astype(jnp.bfloat16)
                         sort_all(stratum + 1)
                         if not first:
+
+                            @pl.when(corner & (stratum == turn))
+                            def clear_row():
+                                move(stratum, 1).wait_send()
+                                clear()
 
                             @pl.when(stop & (stratum == turn))
                             def pass_on():
                                 to_stop().wait_recv()
                                 from_stop().start()
+                                from_stop().wait_send()
+                                clear()
 
     work(jnp.int32(0), True, False)
 
@@ -295,41 +312,30 @@
     lax.fori_loop(1, STRATA - 1, middle, 0)
     work(jnp.int32(STRATA - 1), False, True)
 
-    user_store = pltpu.make_async_copy(user, user_out, factor_sem.at[0])
-    user_store.start()
-    for piece in range(PIECES):
-        rows = slice(piece * width, (piece + 1) * width)
-        pltpu.make_async_copy(
-            fresh.at[STRATA - 1, rows], item_out.at[rows], send_sem.at[STRATA - 1, piece]
-        ).wait()
-
     def sent(stratum, carry):
         @pl.when(jnp.logical_not((stratum == turn - 1) & (place == run - 1)))
         def settle():
-            for piece in range(PIECES):
-                move(stratum, piece).wait_send()
+            move(stratum, 0).wait_send()
+
+            @pl.when(jnp.logical_not((stratum == turn) & corner))
+            def settle_rest():
+                move(stratum, 1).wait_send()
 
         return carry
 
     lax.fori_loop(0, STRATA - 1, sent, 0)
-
-    @pl.when(stop)
-    def settle_passed():
-        from_stop().wait_send()
-
-    user_store.wait()
 
 
 def local(outer_size, inner_size, user_factors, item_factors, ratings, weights, tile_list, tile_count):
     users, strata, items = ratings.shape
     rank = user_factors.shape[1]
     anywhere = pl.BlockSpec(memory_space=pl.ANY)
-    block = jax.ShapeDtypeStruct((users, rank), jnp.float32)
+    block = pltpu.VMEM((users, rank), jnp.float32)
     return pl.pallas_call(
         functools.partial(kernel, outer_size, inner_size),
-        out_shape=(block, jax.ShapeDtypeStruct((items, rank), jnp.float32)),
+        out_shape=(block, pltpu.VMEM((items, rank), jnp.float32)),
         in_specs=[anywhere] * 6,
-        out_specs=(anywhere, anywhere),
+        out_specs=(pl.BlockSpec(memory_space=pltpu.VMEM),) * 2,
         scratch_shapes=[
             pltpu.SMEM((1, tile_list.shape[2], strata), jnp.int32),
             pltpu.SMEM((1, strata), jnp.int32),
@@ -347,11 +353,12 @@
             pltpu.SemaphoreType.DMA((strata, PIECES)),
             pltpu.SemaphoreType.DMA((strata, PIECES)),
             pltpu.SemaphoreType.DMA((2,)),
+            pltpu.SemaphoreType.REGULAR,
         ],
         compiler_params=pltpu.CompilerParams(
             collective_id=0,
             has_side_effects=True,
-            vmem_limit_bytes=60 * 1024 * 1024,
+            vmem_limit_bytes=40 * 1024 * 1024,
         ),
         cost_estimate=pl.CostEstimate(
             flops=3 * 2 * strata * users * items * rank,
@@ -359,12 +366,17 @@
             transcendentals=0,
         ),
     )(
-        jnp.swapaxes(tile_list, 1, 2),
-        tile_count,
-        user_factors,
-        item_factors,
-        ratings.reshape(users * strata, items),
-        weights.reshape(users * strata, items),
+        *[
+            pltpu.with_memory_space_constraint(operand, pltpu.HBM)
+            for operand in (
+                jnp.swapaxes(tile_list, 1, 2),
+                tile_count,
+                user_factors,
+                item_factors,
+                ratings.reshape(users * strata, items),
+                weights.reshape(users * strata, items),
+            )
+        ]
     )
 
 

time: 66 us -> 61.3 us (0.929)
  the two profiles are of different devices: /device:TPU:2 before, /device:TPU:4 now
where the time goes in v3:
time: 61.3 us; the launch traced here: 61.2 us
  Pallas kernels  58.9 us (96%)
  local copies, waits for them, and re-layouts  1.59 us (3%)
  between operations  0.64 us (1%)
    pallas_call x1, Pallas kernels, local(): pl.pallas_call(functools.partial(kernel, outer_size, inner_size), out_sha...  58.9 us
    unnamed x2, local copies, waits for them, and re-layouts  1.59 us

profile of v3, /device:TPU:4, one launch (start us, length us, event | category | flops | bytes accessed | tf_op | source)
XLA Modules:
  0.0 61.2 jit_solution(17536564279524767667)
XLA Ops:
  0.6 58.9 %shard_map.77 = (f32[512,256]{1,0:T(8,128)S(1)}, f32[512,256]{1,0:T(8,128)S(1)}) custom-call(s32[1,4,8]{2,1,0:T(4,128)} %bitcast.5, s32[1,8]{1,0:T(1,128)} %count_hbm.1, f32[512,256]{1,0:T(8,128)} %user_hbm.1, f32[512,256]{1,0:T(8,128)} %item_hbm.1, bf16[4096,512]{1,0:T(8,128)(2,1)} %bitcast.3, bf16[4096,512]{1,0:T(8,128)(2,1)} %bitcast.4), custom_call_target="tpu_custom_call" | custom-call | flops 3221225472 | bytes 10485760 | tf_op jit(solution)/shard_map/pallas_call | solution.py:334
  59.6 0.8 %copy.10 = f32[512,256]{1,0:T(8,128)} copy(f32[512,256]{1,0:T(8,128)S(1)} %get-tuple-element.2) | data formatting | bytes 1048576
  60.4 0.8 %copy.11 = f32[512,256]{1,0:T(8,128)} copy(f32[512,256]{1,0:T(8,128)S(1)} %get-tuple-element.3) | data formatting | bytes 1048576

commit v4 on v3

--- a/solution.py
+++ b/solution.py
@@ -14,7 +14,7 @@
 CHIPS = 4
 CORES = 2
 PIECES = 2
-PARTS = 4
+PARTS = 2
 
 learn_rate = 0.015
 ridge_weight = 0.05
@@ -201,7 +201,7 @@
     def send(stratum, piece):
         if piece == 0:
 
-            @pl.when((stratum == turn) & ((place == run - 2) | (place == run - 4)))
+            @pl.when((stratum == turn) & ((place == run - 4)))
             def hold():
                 pl.semaphore_wait(go_sem, 1)
 
@@ -291,11 +291,6 @@
                         sort_all(stratum + 1)
                         if not first:
 
-                            @pl.when(corner & (stratum == turn))
-                            def clear_row():
-                                move(stratum, 1).wait_send()
-                                clear()
-
                             @pl.when(stop & (stratum == turn))
                             def pass_on():
                                 to_stop().wait_recv()
@@ -315,11 +310,8 @@
     def sent(stratum, carry):
         @pl.when(jnp.logical_not((stratum == turn - 1) & (place == run - 1)))
         def settle():
-            move(stratum, 0).wait_send()
-
-            @pl.when(jnp.logical_not((stratum == turn) & corner))
-            def settle_rest():
-                move(stratum, 1).wait_send()
+            for piece in range(PIECES):
+                move(stratum, piece).wait_send()
 
         return carry
 

time: 61.3 us -> 59.3 us (0.967)
  the two profiles are of different devices: /device:TPU:4 before, /device:TPU:2 now
where the time goes in v4:
time: 59.3 us; the launch traced here: 58.6 us
  Pallas kernels  56.4 us (95%)
  local copies, waits for them, and re-layouts  1.59 us (3%)
  between operations  0.64 us (1%)
    pallas_call x1, Pallas kernels, local(): pl.pallas_call(functools.partial(kernel, outer_size, inner_size), out_sha...  56.4 us
    unnamed x2, local copies, waits for them, and re-layouts  1.59 us

profile of v4, /device:TPU:2, one launch (start us, length us, event | category | flops | bytes accessed | tf_op | source)
XLA Modules:
  0.0 58.6 jit_solution(14998681419260050155)
XLA Ops:
  0.6 56.4 %shard_map.77 = (f32[512,256]{1,0:T(8,128)S(1)}, f32[512,256]{1,0:T(8,128)S(1)}) custom-call(s32[1,4,8]{2,1,0:T(4,128)} %bitcast.5, s32[1,8]{1,0:T(1,128)} %count_hbm.1, f32[512,256]{1,0:T(8,128)} %user_hbm.1, f32[512,256]{1,0:T(8,128)} %item_hbm.1, bf16[4096,512]{1,0:T(8,128)(2,1)} %bitcast.3, bf16[4096,512]{1,0:T(8,128)(2,1)} %bitcast.4), custom_call_target="tpu_custom_call" | custom-call | flops 3221225472 | bytes 10485760 | tf_op jit(solution)/shard_map/pallas_call | solution.py:326
  57.0 0.8 %copy.10 = f32[512,256]{1,0:T(8,128)} copy(f32[512,256]{1,0:T(8,128)S(1)} %get-tuple-element.2) | data formatting | bytes 1048576
  57.8 0.8 %copy.11 = f32[512,256]{1,0:T(8,128)} copy(f32[512,256]{1,0:T(8,128)S(1)} %get-tuple-element.3) | data formatting | bytes 1048576

commit v5 on v4

--- a/solution.py
+++ b/solution.py
@@ -14,7 +14,7 @@
 CHIPS = 4
 CORES = 2
 PIECES = 2
-PARTS = 2
+PARTS = 1
 
 learn_rate = 0.015
 ridge_weight = 0.05

time: 59.3 us -> 58.9 us (level)
  no operation moved by 1% of the time
where the time goes in v5:
time: 58.9 us; the launch traced here: 58.2 us
  Pallas kernels  56 us (95%)
  local copies, waits for them, and re-layouts  1.59 us (3%)
  between operations  0.64 us (1%)
    pallas_call x1, Pallas kernels, local(): pl.pallas_call(functools.partial(kernel, outer_size, inner_size), out_sha...  56 us
    unnamed x2, local copies, waits for them, and re-layouts  1.59 us

profile of v5, /device:TPU:2, one launch (start us, length us, event | category | flops | bytes accessed | tf_op | source)
XLA Modules:
  0.0 58.2 jit_solution(17596293969918014807)
XLA Ops:
  0.6 56.0 %shard_map.77 = (f32[512,256]{1,0:T(8,128)S(1)}, f32[512,256]{1,0:T(8,128)S(1)}) custom-call(s32[1,4,8]{2,1,0:T(4,128)} %bitcast.5, s32[1,8]{1,0:T(1,128)} %count_hbm.1, f32[512,256]{1,0:T(8,128)} %user_hbm.1, f32[512,256]{1,0:T(8,128)} %item_hbm.1, bf16[4096,512]{1,0:T(8,128)(2,1)} %bitcast.3, bf16[4096,512]{1,0:T(8,128)(2,1)} %bitcast.4), custom_call_target="tpu_custom_call" | custom-call | flops 3221225472 | bytes 10485760 | tf_op jit(solution)/shard_map/pallas_call | solution.py:326
  56.6 0.8 %copy.10 = f32[512,256]{1,0:T(8,128)} copy(f32[512,256]{1,0:T(8,128)S(1)} %get-tuple-element.2) | data formatting | bytes 1048576
  57.4 0.8 %copy.11 = f32[512,256]{1,0:T(8,128)} copy(f32[512,256]{1,0:T(8,128)S(1)} %get-tuple-element.3) | data formatting | bytes 1048576
